TPU v7x, 32 devices: a whole 2x2x4 slice. The times are simulated.
32 devices in a mesh: vp: 16 (over z, y, x), red: 2 (over core).
Axes of the slice: x: 2, y: 2, z: 4, core: 2. Of those that a mesh axis runs over, the one named last changes fastest.
Arguments:
- t2_amps: bfloat16 [256, 32768], P('vp', 'red'), may hold values from -6 to 6
- integrals: bfloat16 [32768, 1024], P(('red', 'vp')), may hold values from -0.1875 to 0.1875
- ij_irrep: int32 [256], replicated, may hold values from 0 to 7, as said below
- cd_irrep: int32 [32768], P(('red', 'vp')), may hold values from 0 to 7, as said below
- ab_irrep: int32 [1024], replicated, may hold values from 0 to 7, as said below
Outputs:
- ladder: float32 [256, 1024], P('vp', 'red')
Inputs may be any that keep to these rules, and one draw needn't show every extreme that they name: Most occupied pairs carry one irrep, drawn from the seed and the same for ij_irrep, cd_irrep and ab_irrep; the other pairs are spread over the remaining seven irreps. `cd_irrep`: most contracted pairs carry the common irrep of the three label arrays; the others are spread over the remaining seven irreps. `ab_irrep`: most pairs of the slab carry the common irrep of the three label arrays; the others are spread over the remaining seven irreps.
All inputs are finite; a program needn't handle non-finite values.
Results may differ from a plain program's by a relative error of at most 0.0003.
Values may be sent and summed in bfloat16 or wider, within the bound.
A program may use at most 64 MiB of HBM per device.

v0:
```python
import jax
import jax.numpy as jnp
from jax import lax
from jax.sharding import PartitionSpec as P


def shards(t2_amps, integrals, ij_irrep, cd_irrep, ab_irrep):
    moved = lax.all_to_all(t2_amps, "vp", split_axis=1, concat_axis=0, tiled=True)
    t2_sym = jnp.where(ij_irrep[:, None] == cd_irrep[None, :], moved, jnp.zeros((), moved.dtype))
    v_sym = jnp.where(
        cd_irrep[:, None] == ab_irrep[None, :], integrals, jnp.zeros((), integrals.dtype)
    )
    own_rows = lax.psum_scatter(
        jnp.dot(t2_sym, v_sym, preferred_element_type=jnp.float32),
        "vp",
        scatter_dimension=0,
        tiled=True,
    )
    ladder = lax.psum_scatter(own_rows, "red", scatter_dimension=1, tiled=True)
    return ladder


def solution(mesh):
    placed = (P("vp", "red"), P(("red", "vp"), None), P(), P(("red", "vp")), P())
    return jax.shard_map(
        shards, mesh=mesh, in_specs=placed, out_specs=P("vp", "red"), check_vma=False
    )
```

profile of v0, /device:TPU:0, one launch (start us, length us, event | category | flops | bytes accessed | tf_op | source)
XLA Modules:
  0.0 123.0 jit_solution(10549310957710409030)
XLA Ops:
  6.5 0.0 copy-start.1
  6.5 0.0 copy-start.2
  6.5 0.0 copy-start
  6.5 0.0 reduce-scatter.3.cloned.1.call-start
  6.5 1.2 copy.10
  7.8 23.2 %all_to_all.19 = bf16[16,16,1024]{2,0,1:T(8,128)(2,1)S(1)} all-to-all(bf16[16,16,1024]{2,0,1:T(8,128)(2,1)S(1)} %bitcast.7), channel_id=1, replica_groups=mesh['vp'=16,'red'=2] {'vp'}, dimensions={1} | all-to-all | bytes 1048576 | tf_op jit(solution)/shard_map/all_to_all | solution.py:8
  31.0 0.0 copy-done.1
  31.0 0.0 copy-done.2
  31.0 0.0 copy-done
  31.0 2.7 %fusion = f32[256,1024]{1,0:T(8,128)} fusion(bf16[1024,1024]{1,0:T(8,128)(2,1)S(1)} %copy-done, s32[1024]{0:T(1024)S(1)} %copy-done.1, s32[1024]{0:T(1024)} %param.8, bf16[256,1024]{1,0:T(8,128)(2,1)S(1)} %bitcast.9, s32[256]{0:T(256)S(1)} %copy-done.2), kind=kOutput, calls=%fused_computation.1 | convolution fusion | flops 539492352 | bytes 3679232 | tf_op jit(solution)/shard_map/dot_general | solution.py:14
  33.8 0.0 reduce-scatter.3.cloned.1.call-update
  33.8 0.0 reduce-scatter.5.cloned.1.call-start
  33.9 76.2 %reduce-scatter.3.cloned.1.call-done = f32[16,1024]{1,0:T(8,128)} async-done(((f32[256,1024]{1,0:T(8,128)}), f32[16,1024]{1,0:T(8,128)}) %reduce-scatter.3.cloned.1.call-update) | async-done | bytes 65552 | tf_op jit(solution)/shard_map/reduce_scatter | solution.py:13
  110.0 0.0 reduce-scatter.5.cloned.1.call-update
  110.1 6.1 %reduce-scatter.5.cloned.1.call-done = f32[16,512]{1,0:T(8,128)} async-done(((f32[16,1024]{1,0:T(8,128)}), f32[16,512]{1,0:T(8,128)}) %reduce-scatter.5.cloned.1.call-update) | async-done | bytes 32784 | tf_op jit(solution)/shard_map/reduce_scatter | solution.py:19
Async XLA Ops:
  6.5 24.5 %copy-start.1 = (s32[1024]{0:T(1024)S(1)}, s32[1024]{0:T(1024)}, u32[]{:S(2)}) copy-start(s32[1024]{0:T(1024)} %param.9) | copy-start | bytes 12292
  6.5 24.5 %copy-start.2 = (s32[256]{0:T(256)S(1)}, s32[256]{0:T(256)}, u32[]{:S(2)}) copy-start(s32[256]{0:T(256)} %param.7) | copy-start | bytes 3076
  6.5 24.5 %copy-start = (bf16[1024,1024]{1,0:T(8,128)(2,1)S(1)}, bf16[1024,1024]{1,0:T(8,128)(2,1)}, u32[]{:S(2)}) copy-start(bf16[1024,1024]{1,0:T(8,128)(2,1)} %param.6) | copy-start | bytes 6291460
  6.5 103.5 %reduce-scatter.3.cloned.1.call-start = ((), (), s32[]{:S(2)}) async-start(), calls=%async_computation.3 | async-start | bytes 1114112 | tf_op jit(solution)/shard_map/reduce_scatter | solution.py:13
  33.8 82.3 %reduce-scatter.5.cloned.1.call-start = ((), (), s32[]{:S(2)}) async-start(), calls=%async_computation.4 | async-start | bytes 98304 | tf_op jit(solution)/shard_map/reduce_scatter | solution.py:19
Sparse Core Ops, SparseCore 0:
  33.9 76.0 reduce-scatter.2
  112.3 3.7 reduce-scatter.4
where the time goes:
time: 123 us
  waiting for transfers between devices  82.3 us (67%)
  blocking collectives  23.2 us (19%)
  between operations  13.4 us (11%)
  matrix products  2.74 us (2%)
  local copies, waits for them, and re-layouts  1.24 us (1%)
    reduce_scatter x1, waiting for transfers between devices, shards(): lax.psum_scatter(jnp.dot(t2_sym, v_sym, preferred_element_type=jnp.float3...  76.2 us
    all_to_all x1, blocking collectives, shards(): lax.all_to_all(t2_amps, 'vp', split_axis=1, concat_axis=0, tiled=True)  23.2 us
    reduce_scatter x1, waiting for transfers between devices, shards(): ladder = lax.psum_scatter(own_rows, 'red', scatter_dimension=1, tiled=True)  6.07 us
    dot_general x1, matrix products, shards(): jnp.dot(t2_sym, v_sym, preferred_element_type=jnp.float32)  2.74 us
  transfers between devices with their start and end apart: 2, of which 2 were waited for; matrix products, arithmetic and copies ran while one was open for 0% of the time, Pallas kernels for 0%

commit v1 on v0

v1 whole, which is shorter than its diff:
```python
import functools
import math

import jax
import jax.numpy as jnp
from jax import lax
from jax.experimental import pallas as pl
from jax.experimental.pallas import tpu as pltpu
from jax.sharding import PartitionSpec as P

MESH = pl.DeviceIdType.MESH


def group_of(n):
    size = math.isqrt(n)
    while n % size:
        size -= 1
    return size


def order_of(planes):
    return sorted(range(planes), key=lambda d: (min(d, planes - d), d))


def kernel(
    n, r, size, t_ref, v_ref, ij_hbm, cd_hbm, ab_hbm, out_ref,
    ij_ref, cd_ref, ab_ref, tbuf, vbuf, labels, part, redbuf, own, planebuf, comb, zbuf,
    load_sem, t_send, t_recv, r_send, r_recv, p_send, p_recv, z_send, z_recv,
):
    planes = n // size
    me, core = lax.axis_index("vp"), lax.axis_index("red")
    plane, place = lax.div(me, size), lax.rem(me, size)
    rows, depth = tbuf.shape[1], tbuf.shape[2]
    width = out_ref.shape[1]
    order = order_of(planes)

    def block(who):
        return t_ref.at[:, pl.ds(pl.multiple_of(who * depth, depth), depth)]

    load_v = pltpu.make_async_copy(v_ref, vbuf, load_sem.at[0])
    load_t = pltpu.make_async_copy(block(me), tbuf.at[me], load_sem.at[1])
    load_labels = [
        pltpu.make_async_copy(src, dst, load_sem.at[2 + i])
        for i, (src, dst) in enumerate(
            [(ij_hbm, ij_ref), (cd_hbm, cd_ref), (ab_hbm, ab_ref)]
        )
    ]
    for copy in (load_t, *load_labels, load_v):
        copy.start()

    barrier = pltpu.get_barrier_semaphore()
    for d in range(1, n):
        pl.semaphore_signal(
            barrier, inc=1, device_id=(lax.rem(me + d, n), core), device_id_type=MESH
        )
    for d in range(1, r):
        pl.semaphore_signal(
            barrier, inc=1, device_id=(me, lax.rem(core + d, r)), device_id_type=MESH
        )
    pl.semaphore_wait(barrier, n - 1 + r - 1)

    t_copies = {}
    for dz in order:
        for dp in range(size):
            if dz == 0 and dp == 0:
                continue
            who = lax.rem(plane + dz, planes) * size + lax.rem(place + dp, size)
            copy = pltpu.make_async_remote_copy(
                src_ref=block(who),
                dst_ref=tbuf.at[me],
                send_sem=t_send.at[dz, dp],
                recv_sem=t_recv.at[dz, dp],
                device_id=(who, core),
                device_id_type=MESH,
            )
            copy.start()
            t_copies[dz, dp] = copy

    for copy in load_labels:
        copy.wait()
    labels[...] = jnp.transpose(jnp.broadcast_to(ij_ref[...], (128, ij_ref.shape[1])))
    load_t.wait()
    load_v.wait()

    sent = []

    def multiply(step):
        dz = order[step]
        for dp in range(size):
            if (dz, dp) in t_copies:
                t_copies[dz, dp].wait_recv()
        source = lax.rem(plane + planes - dz, planes)
        amps = tbuf[pl.ds(source * size, size)].reshape(size * rows, depth)
        first = pl.multiple_of(source * (size * rows), size * rows)
        kept = labels[pl.ds(first, size * rows), :][:, :1] == cd_ref[...]
        amps = jnp.where(kept, amps.astype(jnp.float32), 0.0).astype(amps.dtype)
        copies = []
        for d in [*range(1, r), 0]:
            to = lax.rem(core + d, r)
            columns = pl.ds(pl.multiple_of(to * width, width), width)
            part[step, d] = jnp.dot(
                amps, vbuf[:, columns], preferred_element_type=jnp.float32
            )
            if d:
                copy = pltpu.make_async_remote_copy(
                    src_ref=part.at[step, d],
                    dst_ref=redbuf.at[step, d - 1],
                    send_sem=r_send.at[step, d - 1],
                    recv_sem=r_recv.at[step, d - 1],
                    device_id=(me, to),
                    device_id_type=MESH,
                )
                copy.start()
                copies.append(copy)
                sent.append(copy)
        return copies

    def spread(step, copies):
        total = part[step, 0]
        for d, copy in enumerate(copies):
            copy.wait_recv()
            total = total + redbuf[step, d]
        own[step] = total.reshape(size, rows, width)
        out = []
        for d in range(1, size):
            to = lax.rem(place + d, size)
            copy = pltpu.make_async_remote_copy(
                src_ref=own.at[step, to],
                dst_ref=planebuf.at[step, d - 1],
                send_sem=p_send.at[step, d - 1],
                recv_sem=p_recv.at[step, d - 1],
                device_id=(plane * size + to, core),
                device_id_type=MESH,
            )
            copy.start()
            out.append(copy)
            sent.append(copy)
        return out

    def gather(step, copies):
        total = own[step, place]
        for d, copy in enumerate(copies):
            copy.wait_recv()
            total = total + planebuf[step, d]
        comb[step] = total
        if step == 0:
            return None
        owner = lax.rem(plane + planes - order[step], planes)
        copy = pltpu.make_async_remote_copy(
            src_ref=comb.at[step],
            dst_ref=zbuf.at[step - 1],
            send_sem=z_send.at[step - 1],
            recv_sem=z_recv.at[step - 1],
            device_id=(owner * size + place, core),
            device_id_type=MESH,
        )
        copy.start()
        sent.append(copy)
        return copy

    last, finals = None, []
    for step in range(planes):
        copies = multiply(step)
        if last is not None:
            finals.append(gather(step - 1, last))
        last = spread(step, copies)
    finals.append(gather(planes - 1, last))

    total = comb[0]
    for step in range(1, planes):
        finals[step].wait_recv()
        total = total + zbuf[step - 1]
    mine = labels[pl.ds(pl.multiple_of(me * rows, rows), rows), :][:, :1]
    theirs = ab_ref[:, pl.ds(pl.multiple_of(core * width, width), width)]
    out_ref[...] = jnp.where(mine == theirs, total, 0.0)

    for copy in [*t_copies.values(), *sent]:
        copy.wait_send()


def shards(n, r, t2_amps, integrals, ij_irrep, cd_irrep, ab_irrep):
    rows = t2_amps.shape[0]
    depth, wide = integrals.shape
    width = wide // r
    size = group_of(n)
    planes = n // size
    f32 = jnp.float32
    dma = pltpu.SemaphoreType.DMA
    vmem = pl.BlockSpec(memory_space=pltpu.VMEM)
    hbm = pl.BlockSpec(memory_space=pltpu.HBM)
    return pl.pallas_call(
        functools.partial(kernel, n, r, size),
        out_shape=jax.ShapeDtypeStruct((rows, width), f32),
        in_specs=[hbm] * 5,
        out_specs=vmem,
        scratch_shapes=[
            pltpu.VMEM((1, n * rows), jnp.int32),
            pltpu.VMEM((1, depth), jnp.int32),
            pltpu.VMEM((1, wide), jnp.int32),
            pltpu.VMEM((n, rows, depth), t2_amps.dtype),
            pltpu.VMEM((depth, wide), integrals.dtype),
            pltpu.VMEM((n * rows, 128), jnp.int32),
            pltpu.VMEM((planes, r, size * rows, width), f32),
            pltpu.VMEM((planes, max(r - 1, 1), size * rows, width), f32),
            pltpu.VMEM((planes, size, rows, width), f32),
            pltpu.VMEM((planes, max(size - 1, 1), rows, width), f32),
            pltpu.VMEM((planes, rows, width), f32),
            pltpu.VMEM((max(planes - 1, 1), rows, width), f32),
            dma((5,)),
            dma((planes, size)),
            dma((planes, size)),
            dma((planes, max(r - 1, 1))),
            dma((planes, max(r - 1, 1))),
            dma((planes, max(size - 1, 1))),
            dma((planes, max(size - 1, 1))),
            dma((max(planes - 1, 1),)),
            dma((max(planes - 1, 1),)),
        ],
        cost_estimate=pl.CostEstimate(
            flops=2 * n * rows * depth * wide,
            bytes_accessed=2 * (n * rows * depth + depth * wide) + 4 * rows * width,
            transcendentals=0,
        ),
        compiler_params=pltpu.CompilerParams(
            collective_id=0, has_side_effects=True, vmem_limit_bytes=60 * 2**20
        ),
    )(t2_amps, integrals, ij_irrep[None, :], cd_irrep[None, :], ab_irrep[None, :])


def solution(mesh):
    placed = (P("vp", "red"), P(("red", "vp"), None), P(), P(("red", "vp")), P())
    return jax.shard_map(
        functools.partial(shards, mesh.shape["vp"], mesh.shape["red"]),
        mesh=mesh,
        in_specs=placed,
        out_specs=P("vp", "red"),
        check_vma=False,
    )
```

time: 123 us -> 36.6 us (0.30)
  waiting for transfers between devices: 82.3 us -> 0 us
  Pallas kernels: 0 us -> 35.1 us
  blocking collectives: 23.2 us -> 0 us
  between operations: 13.4 us -> 0.01 us
  matrix products: 2.74 us -> 0 us
    reduce_scatter x2 -> x0, waiting for transfers between devices: 82.2 us -> none  [the longest x1 76.2 us: shards(): lax.psum_scatter(jnp.dot(t2_sym, v_sym, preferred_element_type=jnp.float3...]
    pallas_call x0 -> x1, Pallas kernels: none -> 35.1 us  [shards(): pl.pallas_call(functools.partial(kernel, n, r, size), out_shape=jax.Shape...]
    all_to_all x1 -> x0, blocking collectives: 23.2 us -> none  [shards(): lax.all_to_all(t2_amps, 'vp', split_axis=1, concat_axis=0, tiled=True)]
    dot_general x1 -> x0, matrix products: 2.74 us -> none  [shards(): jnp.dot(t2_sym, v_sym, preferred_element_type=jnp.float32)]
    unnamed x6 -> x1, local copies, waits for them, and re-layouts: 0.01 us -> 1.38 us
  transfers between devices with their start and end apart: 2 -> 0, of which waited for: 2 -> 0; matrix products, arithmetic and copies ran while one was open for 0% -> 0% of each run, Pallas kernels for 0% -> 0%
where the time goes in v1:
time: 36.6 us; the launch traced here: 36.5 us
  Pallas kernels  35.1 us (96%)
  local copies, waits for them, and re-layouts  1.38 us (4%)
    pallas_call x1, Pallas kernels, shards(): pl.pallas_call(functools.partial(kernel, n, r, size), out_shape=jax.Shape...  35.1 us
    unnamed x1, local copies, waits for them, and re-layouts  1.38 us

profile of v1, /device:TPU:0, one launch (start us, length us, event | category | flops | bytes accessed | tf_op | source)
XLA Modules:
  0.0 36.5 jit_solution(1750534084228021053)
XLA Ops:
  0.0 35.1 %shard_map.55 = f32[16,512]{1,0:T(8,128)} custom-call(bf16[16,16384]{1,0:T(8,128)(2,1)} %t_ref.1, bf16[1024,1024]{1,0:T(8,128)(2,1)} %v_ref.1, s32[1,256]{1,0:T(1,128)} %bitcast.5, s32[1,1024]{1,0:T(1,128)} %bitcast.3, s32[1,1024]{1,0:T(1,128)} %bitcast.4), custom_call_target="tpu_custom_call" | custom-call | flops 536870912 | bytes 2654208 | tf_op jit(solution)/shard_map/pallas_call | solution.py:191
  35.1 1.4 %copy.7 = f32[16,512]{1,0:T(8,128)} copy(f32[16,512]{1,0:T(8,128)} %shard_map.55) | data formatting | bytes 65536

commit v2 on v1

--- a/solution.py
+++ b/solution.py
@@ -19,7 +19,7 @@
 
 
 def order_of(planes):
-    return sorted(range(planes), key=lambda d: (min(d, planes - d), d))
+    return [0, *sorted(range(1, planes), key=lambda d: (-min(d, planes - d), -d))]
 
 
 def kernel(
@@ -143,14 +143,15 @@
             copy.wait_recv()
             total = total + planebuf[step, d]
         comb[step] = total
-        if step == 0:
+        dz = order[step]
+        if dz == 0:
             return None
-        owner = lax.rem(plane + planes - order[step], planes)
+        owner = lax.rem(plane + planes - dz, planes)
         copy = pltpu.make_async_remote_copy(
             src_ref=comb.at[step],
-            dst_ref=zbuf.at[step - 1],
-            send_sem=z_send.at[step - 1],
-            recv_sem=z_recv.at[step - 1],
+            dst_ref=zbuf.at[dz - 1],
+            send_sem=z_send.at[dz - 1],
+            recv_sem=z_recv.at[dz - 1],
             device_id=(owner * size + place, core),
             device_id_type=MESH,
         )
@@ -166,10 +167,11 @@
         last = spread(step, copies)
     finals.append(gather(planes - 1, last))
 
-    total = comb[0]
-    for step in range(1, planes):
-        finals[step].wait_recv()
-        total = total + zbuf[step - 1]
+    total = comb[order.index(0)]
+    for step, dz in enumerate(order):
+        if dz:
+            finals[step].wait_recv()
+            total = total + zbuf[dz - 1]
     mine = labels[pl.ds(pl.multiple_of(me * rows, rows), rows), :][:, :1]
     theirs = ab_ref[:, pl.ds(pl.multiple_of(core * width, width), width)]
     out_ref[...] = jnp.where(mine == theirs, total, 0.0)

time: 36.6 us -> 34.1 us (0.932)
  Pallas kernels: 35.1 us -> 32.5 us
    pallas_call x1, Pallas kernels: 35.1 us -> 32.5 us  [shards(): pl.pallas_call(functools.partial(kernel, n, r, size), out_shape=jax.Shape...]
where the time goes in v2:
time: 34.1 us; the launch traced here: 33.9 us
  Pallas kernels  32.5 us (95%)
  local copies, waits for them, and re-layouts  1.38 us (4%)
    pallas_call x1, Pallas kernels, shards(): pl.pallas_call(functools.partial(kernel, n, r, size), out_shape=jax.Shape...  32.5 us
    unnamed x1, local copies, waits for them, and re-layouts  1.38 us

profile of v2, /device:TPU:0, one launch (start us, length us, event | category | flops | bytes accessed | tf_op | source)
XLA Modules:
  0.0 33.9 jit_solution(13009192985431971035)
XLA Ops:
  0.0 32.5 %shard_map.55 = f32[16,512]{1,0:T(8,128)} custom-call(bf16[16,16384]{1,0:T(8,128)(2,1)} %t_ref.1, bf16[1024,1024]{1,0:T(8,128)(2,1)} %v_ref.1, s32[1,256]{1,0:T(1,128)} %bitcast.5, s32[1,1024]{1,0:T(1,128)} %bitcast.3, s32[1,1024]{1,0:T(1,128)} %bitcast.4), custom_call_target="tpu_custom_call" | custom-call | flops 536870912 | bytes 2654208 | tf_op jit(solution)/shard_map/pallas_call | solution.py:193
  32.5 1.4 %copy.7 = f32[16,512]{1,0:T(8,128)} copy(f32[16,512]{1,0:T(8,128)} %shard_map.55) | data formatting | bytes 65536

commit v3 on v2

--- a/solution.py
+++ b/solution.py
@@ -161,10 +161,10 @@
 
     last, finals = None, []
     for step in range(planes):
-        copies = multiply(step)
+        here = spread(step, multiply(step))
         if last is not None:
             finals.append(gather(step - 1, last))
-        last = spread(step, copies)
+        last = here
     finals.append(gather(planes - 1, last))
 
     total = comb[order.index(0)]

time: 34.1 us -> 32.3 us (0.947)
  Pallas kernels: 32.5 us -> 30.7 us
    pallas_call x1, Pallas kernels: 32.5 us -> 30.7 us  [shards(): pl.pallas_call(functools.partial(kernel, n, r, size), out_shape=jax.Shape...]
where the time goes in v3:
time: 32.3 us; the launch traced here: 32.1 us
  Pallas kernels  30.7 us (95%)
  local copies, waits for them, and re-layouts  1.38 us (4%)
    pallas_call x1, Pallas kernels, shards(): pl.pallas_call(functools.partial(kernel, n, r, size), out_shape=jax.Shape...  30.7 us
    unnamed x1, local copies, waits for them, and re-layouts  1.38 us

profile of v3, /device:TPU:0, one launch (start us, length us, event | category | flops | bytes accessed | tf_op | source)
XLA Modules:
  0.0 32.1 jit_solution(11319291231808226098)
XLA Ops:
  0.0 30.7 %shard_map.55 = f32[16,512]{1,0:T(8,128)} custom-call(bf16[16,16384]{1,0:T(8,128)(2,1)} %t_ref.1, bf16[1024,1024]{1,0:T(8,128)(2,1)} %v_ref.1, s32[1,256]{1,0:T(1,128)} %bitcast.5, s32[1,1024]{1,0:T(1,128)} %bitcast.3, s32[1,1024]{1,0:T(1,128)} %bitcast.4), custom_call_target="tpu_custom_call" | custom-call | flops 536870912 | bytes 2654208 | tf_op jit(solution)/shard_map/pallas_call | solution.py:193
  30.7 1.4 %copy.7 = f32[16,512]{1,0:T(8,128)} copy(f32[16,512]{1,0:T(8,128)} %shard_map.55) | data formatting | bytes 65536
